TPU v7x, 512 devices: a whole 4x4x16 slice. The times are simulated.
512 devices in a mesh: tm: 32 (over z, core), row: 16 (over y, x).
Axes of the slice: x: 4, y: 4, z: 16, core: 2. Of those that a mesh axis runs over, the one named last changes fastest.
Arguments:
- covariance: float32 [32, 1024, 1024], P('tm', 'row'), as said below
- precision: float32 [32, 1024, 1024], P('tm', 'row'), as said below
- band_weight: float32 [32, 5, 1024], P('tm'), may hold values from -0.5 to 0.5
- band_offset: int32 [32, 5], P('tm'), may hold values from -64 to 64, as said below
- prior_mean: float32 [32, 1024], P('tm', 'row'), may hold values from -6 to 6
- innovation: float32 [32, 128], P('tm'), may hold values from -6 to 6
- seen_sites: int32 [32, 128], P('tm'), may hold values from 0 to 511, as said below
Outputs:
- smoother_gain: float32 [32, 1024, 1024], P('tm', 'row')
- smoother_shift: float32 [32, 1024], P('tm', 'row')
- smoother_spread: float32 [32, 1024, 1024], P('tm', 'row')
Inputs may be any that keep to these rules, and one draw needn't show every extreme that they name: `covariance`: each block's matrix is symmetric. `precision`: each block's matrix is symmetric. `band_offset`: the offsets of one block are distinct, and one of them has magnitude 64. `seen_sites`: the sites of one step are distinct.
All inputs are finite; a program needn't handle non-finite values.
Results may differ from a plain program's by a relative error of at most 0.0003.
Values sent between devices are 32-bit elements; how exact they have to be, the bound alone decides.
No kernel may reach another device: no remote copies, remote signals or barrier semaphores. Data moves between devices by JAX's collectives and lax.ppermute only.
A program may use at most 64 MiB of HBM per device.

v0:
```python
import jax
import jax.numpy as jnp
from jax import lax
from jax.sharding import PartitionSpec as P

NBAND = 5
REACH = 64
HIGHEST = lax.Precision.HIGHEST


def padded_2(cells, sides, width):
    for axis, dim in sides:
        count = lax.axis_size(axis)
        ends = count - 1
        head = lax.slice_in_dim(cells, 0, width, axis=dim)
        tail = lax.slice_in_dim(cells, cells.shape[dim] - width, cells.shape[dim], axis=dim)
        cells = jnp.concatenate(
            [
                lax.ppermute(tail, axis, [(i, (i + 1) % count) for i in range(ends)]),
                cells,
                lax.ppermute(head, axis, [((i + 1) % count, i) for i in range(ends)]),
            ],
            axis=dim,
        )
    return cells


def shifted(block, axis, distance):
    devices = range(lax.axis_size(axis))
    route = [(i - distance, i) for i in devices if i - distance in devices]
    return lax.ppermute(block, axis, route)


def product(left, right):
    return jnp.dot(left, right, precision=HIGHEST, preferred_element_type=jnp.float32)


def against(left, right):
    return lax.dot_general(
        left, right, (((1,), (1,)), ((), ())), precision=HIGHEST, preferred_element_type=jnp.float32
    )


def band_columns(matrix, weights, offsets):
    columns = matrix.shape[1]
    padded = jnp.pad(matrix, ((0, 0), (REACH, REACH)))
    summed = jnp.zeros(matrix.shape, jnp.float32)
    for band_index in range(NBAND):
        start_at = offsets[band_index] + REACH
        sliced = lax.dynamic_slice_in_dim(padded, start_at, columns, 1)
        summed = summed + weights[band_index][None, :] * sliced
    return summed


def body(covariance, precision, band_weight, band_offset, prior_mean, innovation, seen_sites):
    spread_rows = covariance[0]
    weights = band_weight[0]
    offsets = band_offset[0]
    local_rows = spread_rows.shape[0]
    columns = spread_rows.shape[1]
    first_local = lax.axis_index("row") * local_rows
    crossed = band_columns(spread_rows, weights, offsets)
    gain_rows = product(crossed, lax.all_gather(precision[0], "row", axis=0, tiled=True))
    matches = (seen_sites[0][:, None] == jnp.arange(columns, dtype=jnp.int32)[None, :]).astype(
        jnp.float32
    )
    pulled = product(innovation[0], matches)
    filtered = prior_mean[0] + product(spread_rows, pulled)
    rimmed = padded_2(filtered, (("row", 0),), REACH)
    local_weights = lax.dynamic_slice_in_dim(weights, first_local, local_rows, 1)
    forward = jnp.zeros((local_rows,), jnp.float32)
    for band_index in range(NBAND):
        start_at = offsets[band_index] + REACH
        forward = forward + local_weights[band_index] * lax.dynamic_slice_in_dim(
            rimmed, start_at, local_rows, 0
        )
    gain_full, forward_full = (
        lax.all_gather(gain_rows, "row", axis=0, tiled=True),
        lax.all_gather(forward, "row", axis=0, tiled=True),
    )
    spread_now = spread_rows - against(crossed, gain_full)
    shift_rows = filtered - product(gain_rows, forward_full)
    time_index = lax.axis_index("tm")
    time_count = lax.axis_size("tm")
    for stride in (1, 2):
        piece_gain, piece_shift, piece_spread = shifted(
            (gain_rows, shift_rows, spread_now), "tm", -stride
        )
        later_gain, later_shift, later_spread = (
            lax.all_gather(piece_gain, "row", axis=0, tiled=True),
            lax.all_gather(piece_shift, "row", axis=0, tiled=True),
            lax.all_gather(piece_spread, "row", axis=0, tiled=True),
        )
        merged_gain = product(gain_rows, later_gain)
        merged_shift = product(gain_rows, later_shift) + shift_rows
        merged_spread = against(product(gain_rows, later_spread), gain_full) + spread_now
        inside = time_index + stride < time_count
        if stride == 1:
            gain_full = jnp.where(inside, product(gain_full, later_gain), gain_full)
        gain_rows = jnp.where(inside, merged_gain, gain_rows)
        shift_rows = jnp.where(inside, merged_shift, shift_rows)
        spread_now = jnp.where(inside, merged_spread, spread_now)
    return (gain_rows[None], shift_rows[None], spread_now[None])


def solution(mesh):
    in_specs = (
        P("tm", "row", None),
        P("tm", "row", None),
        P("tm", None, None),
        P("tm", None),
        P("tm", "row"),
        P("tm", None),
        P("tm", None),
    )
    out_specs = (P("tm", "row", None), P("tm", "row"), P("tm", "row", None))
    return jax.shard_map(body, mesh=mesh, in_specs=in_specs, out_specs=out_specs, check_vma=False)
```

profile of v0, /device:TPU:96, one launch (start us, length us, event | category | flops | bytes accessed | tf_op | source)
XLA Modules:
  0.0 491.6 jit_solution(2502290297912747095)
XLA Ops:
  18.5 62.7 %all-gather.18.cloned.1.call-done = f32[1,1024,1024]{2,1,0:T(8,128)} async-done(((f32[1,64,1024]{2,1,0:T(8,128)}), f32[1,1024,1024]{2,1,0:T(8,128)}) %all-gather.18.cloned.1.call-update) | async-done | bytes 4194320 | tf_op jit(solution)/shard_map/all_gather | solution.py:63
  81.3 5.5 %fusion = f32[64,1024]{1,0:T(8,128)} fusion(f32[64,1024]{1,0:T(8,128)S(1)} %fusion.27, f32[1,1024,1024]{2,1,0:T(8,128)} %all-gather.18.cloned.1.call-done), kind=kOutput, calls=%fused_computation | convolution fusion | flops 805306368 | bytes 4718592 | tf_op jit(solution)/shard_map/dot_general | solution.py:35
  88.8 4.2 collective-permute-done
  93.8 59.8 %all-gather.12.cloned.1.call-done = f32[1024,1024]{1,0:T(8,128)} async-done(((f32[64,1024]{1,0:T(8,128)}), f32[1024,1024]{1,0:T(8,128)}) %all-gather.12.cloned.1.call-update) | async-done | bytes 4194320 | tf_op jit(solution)/shard_map/all_gather | solution.py:78
  153.6 6.3 %convolution_subtract_fusion = f32[64,1024]{1,0:T(8,128)S(1)} fusion(f32[64,1024]{1,0:T(8,128)S(1)} %fusion.27, f32[1024,1024]{1,0:T(8,128)} %all-gather.12.cloned.1.call-done, f32[1,64,1024]{2,1,0:T(8,128)S(1)} %copy-done.4), kind=kOutput, calls=%fused_computation.10 | convolution fusion | flops 805371904 | bytes 4980736 | tf_op jit(solution)/shard_map/dot_general | solution.py:39
  161.8 3.9 collective-permute-done.6
  166.5 57.4 %all-gather.8.cloned.1.call-done = f32[1024,1024]{1,0:T(8,128)} async-done(((f32[64,1024]{1,0:T(8,128)}), f32[1024,1024]{1,0:T(8,128)}) %all-gather.8.cloned.1.call-update) | async-done | bytes 4194320 | tf_op jit(solution)/shard_map/all_gather | solution.py:90
  223.9 4.8 convolution_select_fusion.1
  228.7 2.4 collective-permute-start.1
  231.1 8.8 %collective-permute-done.1 = f32[64,1024]{1,0:T(8,128)S(1)} collective-permute-done((f32[64,1024]{1,0:T(8,128)S(1)}, f32[64,1024]{1,0:T(8,128)S(1)}, u32[]{:S(2)}, u32[]{:S(2)}) %collective-permute-start.1) | collective-permute-done | bytes 262176 | tf_op jit(solution)/shard_map/ppermute | solution.py:31
  240.9 52.5 %all-gather.14.cloned.1.call-done = f32[1024,1024]{1,0:T(8,128)} async-done(((f32[64,1024]{1,0:T(8,128)}), f32[1024,1024]{1,0:T(8,128)}) %all-gather.14.cloned.1.call-update) | async-done | bytes 4194320 | tf_op jit(solution)/shard_map/all_gather | solution.py:92
  293.4 5.0 %fusion.52 = f32[64,1024]{1,0:T(8,128)S(1)} fusion(f32[64,1024]{1,0:T(8,128)S(1)} %copy-done.3, f32[1024,1024]{1,0:T(8,128)} %all-gather.14.cloned.1.call-done), kind=kOutput, calls=%fused_computation.67 | convolution fusion | flops 805306368 | bytes 4718592 | tf_op jit(solution)/shard_map/dot_general | solution.py:35
  298.4 4.1 fusion.6
  302.5 2.4 collective-permute-start.7
  304.9 8.8 %collective-permute-done.7 = f32[64,1024]{1,0:T(8,128)S(1)} collective-permute-done((f32[64,1024]{1,0:T(8,128)S(1)}, f32[64,1024]{1,0:T(8,128)S(1)}, u32[]{:S(2)}, u32[]{:S(2)}) %collective-permute-start.7) | collective-permute-done | bytes 262176 | tf_op jit(solution)/shard_map/ppermute | solution.py:31
  316.4 4.5 collective-permute-start.2
  327.1 37.3 %all-reduce.1 = f32[1024]{0:T(1024)S(1)} all-reduce(f32[1024]{0:T(1024)S(1)} %fusion.37), channel_id=1, replica_groups=mesh['tm'=32,'row'=16] {'row'}, use_global_device_ids=true, to_apply=%add.1 | all-reduce | flops 1024 | bytes 8192
  368.1 36.0 %all-reduce.2 = f32[1024]{0:T(1024)S(1)} all-reduce(f32[1024]{0:T(1024)S(1)} %dynamic-update-slice.1), channel_id=1, replica_groups=mesh['tm'=32,'row'=16] {'row'}, use_global_device_ids=true, to_apply=%add.2 | all-reduce | flops 1024 | bytes 8192
  406.4 4.7 collective-permute-done.5
  411.3 37.4 %all-reduce.3 = f32[1024]{0:T(1024)S(1)} all-reduce(f32[1024]{0:T(1024)S(1)} %dynamic-update-slice.2), channel_id=1, replica_groups=mesh['tm'=32,'row'=16] {'row'}, use_global_device_ids=true, to_apply=%add.3 | all-reduce | flops 1024 | bytes 8192
  449.5 17.5 %fusion.54 = f32[1024,1024]{1,0:T(8,128)} fusion(f32[1024,1024]{1,0:T(8,128)} %all-gather.12.cloned.1.call-done, f32[1024,1024]{1,0:T(8,128)} %all-gather.8.cloned.1.call-done), kind=kOutput, calls=%fused_computation.69 | convolution fusion | flops 12884901888 | bytes 12582912 | tf_op jit(solution)/shard_map/dot_general | solution.py:35
  467.0 5.5 %fusion.5 = f32[1,64,1024]{2,1,0:T(8,128)} fusion(f32[64,1024]{1,0:T(8,128)S(1)} %convolution_select_fusion.1, f32[1024,1024]{1,0:T(8,128)} %all-gather.10.cloned.1.call-done, pred[]{:T(512)S(6)} %lt.29), kind=kOutput, calls=%fused_computation.7 | convolution fusion | flops 805371904 | bytes 4718593 | tf_op jit(solution)/shard_map/dot_general | solution.py:35
  472.6 5.0 %fusion.53 = f32[64,1024]{1,0:T(8,128)S(1)} fusion(f32[64,1024]{1,0:T(8,128)S(1)} %convolution_select_fusion.1, f32[1024,1024]{1,0:T(8,128)} %all-gather.16.cloned.1.call-done), kind=kOutput, calls=%fused_computation.68 | convolution fusion | flops 805306368 | bytes 4718592 | tf_op jit(solution)/shard_map/dot_general | solution.py:35
  477.6 7.2 %fusion.13 = f32[1,64,1024]{2,1,0:T(8,128)} fusion(f32[64,1024]{1,0:T(8,128)S(1)} %fusion.6, f32[64,1024]{1,0:T(8,128)S(1)} %fusion.53, f32[1024,1024]{1,0:T(8,128)} %fusion.54, f32[1024,1024]{1,0:T(8,128)S(1)} %copy-done.2, pred[]{:T(512)S(6)} %lt.30, pred[]{:T(512)S(6)} %lt.29), kind=kOutput, calls=%fused_computation.13 | convolution fusion | flops 806486016 | bytes 9175042 | tf_op jit(solution)/shard_map/dot_general | solution.py:39
  (60 shorter events, 23.1 us)
Async XLA Ops:
  7.2 307.3 %copy-start = (f32[1,128]{1,0:T(1,128)S(1)}, f32[1,128]{1,0:T(1,128)}, u32[]{:S(2)}) copy-start(f32[1,128]{1,0:T(1,128)} %param.12) | copy-start | bytes 1540
  7.2 146.5 %copy-start.4 = (f32[1,64,1024]{2,1,0:T(8,128)S(1)}, f32[1,64,1024]{2,1,0:T(8,128)}, u32[]{:S(2)}) copy-start(f32[1,64,1024]{2,1,0:T(8,128)} %param.7) | copy-start | bytes 786436
  7.2 74.1 %all-gather.18.cloned.1.call-start = ((), (), s32[]{:S(2)}) async-start(), calls=%async_computation.5 | async-start | bytes 4456448 | tf_op jit(solution)/shard_map/all_gather | solution.py:63
  7.9 145.7 %all-gather.12.cloned.1.call-start = ((), (), s32[]{:S(2)}) async-start(), calls=%async_computation.2 | async-start | bytes 4456448 | tf_op jit(solution)/shard_map/all_gather | solution.py:78
  86.8 137.1 %copy-start.3 = (f32[64,1024]{1,0:T(8,128)S(1)}, f32[64,1024]{1,0:T(8,128)}, u32[]{:S(2)}) copy-start(f32[64,1024]{1,0:T(8,128)} %fusion) | copy-start | bytes 786436
  86.9 137.0 %all-gather.8.cloned.1.call-start = ((), (), s32[]{:S(2)}) async-start(), calls=%async_computation | async-start | bytes 4456448 | tf_op jit(solution)/shard_map/all_gather | solution.py:90
  86.9 6.1 %collective-permute-start = (f32[64,1024]{1,0:T(8,128)}, f32[64,1024]{1,0:T(8,128)S(1)}, u32[]{:S(2)}, u32[]{:S(2)}) collective-permute-start(f32[64,1024]{1,0:T(8,128)} %fusion), channel_id=1, source_target_pairs={{16,0},{32,16},{48,32},{64,48},{80,64},{96,80},{112,96},{128,112},... | collective-permute-start | bytes 786440 | tf_op jit(solution)/shard_map/ppermute | solution.py:31
  93.7 199.7 %all-gather.14.cloned.1.call-start = ((), (), s32[]{:S(2)}) async-start(), calls=%async_computation.3 | async-start | bytes 4456448 | tf_op jit(solution)/shard_map/all_gather | solution.py:92
  159.9 5.8 %collective-permute-start.6 = (f32[64,1024]{1,0:T(8,128)S(1)}, f32[64,1024]{1,0:T(8,128)S(1)}, u32[]{:S(2)}, u32[]{:S(2)}) collective-permute-start(f32[64,1024]{1,0:T(8,128)S(1)} %convolution_subtract_fusion), channel_id=1, source_target_pairs={{16,0},{32,16},{48,32},{64,48},{80,64},{96,80},{112,96},{128,112},... | collective-permute-start | bytes 786440 | tf_op jit(solution)/shard_map/ppermute | solution.py:31
  165.7 0.7 copy-start.8
  166.4 300.6 %all-gather.10.cloned.1.call-start = ((), (), s32[]{:S(2)}) async-start(), calls=%async_computation.1 | async-start | bytes 4456448 | tf_op jit(solution)/shard_map/all_gather | solution.py:90
  228.7 11.2 %collective-permute-start.1 = (f32[64,1024]{1,0:T(8,128)S(1)}, f32[64,1024]{1,0:T(8,128)S(1)}, u32[]{:S(2)}, u32[]{:S(2)}) collective-permute-start(f32[64,1024]{1,0:T(8,128)S(1)} %convolution_select_fusion.1), channel_id=1, source_target_pairs={{32,0},{48,16},{64,32},{80,48},{96,64},{112,80},{128,96},{144,112}... | collective-permute-start | bytes 786440 | tf_op jit(solution)/shard_map/ppermute | solution.py:31
  239.9 0.7 copy-start.5
  240.6 73.8 %copy-start.10 = (s32[1,128]{1,0:T(1,128)S(1)}, s32[1,128]{1,0:T(1,128)}, u32[]{:S(2)}) copy-start(s32[1,128]{1,0:T(1,128)} %param.13) | copy-start | bytes 1540
  240.6 74.1 %copy-start.9 = (f32[1,64]{1,0:T(1,128)S(1)}, f32[1,64]{1,0:T(1,128)}, u32[]{:S(2)}) copy-start(f32[1,64]{1,0:T(1,128)} %param.11) | copy-start | bytes 772
  240.6 231.9 %all-gather.16.cloned.1.call-start = ((), (), s32[]{:S(2)}) async-start(), calls=%async_computation.4 | async-start | bytes 4456448 | tf_op jit(solution)/shard_map/all_gather | solution.py:92
  293.4 5.0 %copy-start.1 = (f32[1024,1024]{1,0:T(8,128)S(1)}, f32[1024,1024]{1,0:T(8,128)}, u32[]{:S(2)}) copy-start(f32[1024,1024]{1,0:T(8,128)} %all-gather.12.cloned.1.call-done) | copy-start | bytes 12582916
  302.5 11.1 %collective-permute-start.7 = (f32[64,1024]{1,0:T(8,128)S(1)}, f32[64,1024]{1,0:T(8,128)S(1)}, u32[]{:S(2)}, u32[]{:S(2)}) collective-permute-start(f32[64,1024]{1,0:T(8,128)S(1)} %fusion.6), channel_id=1, source_target_pairs={{32,0},{48,16},{64,32},{80,48},{96,64},{112,80},{128,96},{144,112}... | collective-permute-start | bytes 786440 | tf_op jit(solution)/shard_map/ppermute | solution.py:31
  313.7 0.7 copy-start.6
  315.1 11.1 %collective-permute-start.3 = (f32[64]{0:T(128)S(1)}, f32[64]{0:T(128)S(1)}, u32[]{:S(2)}, u32[]{:S(2)}) collective-permute-start(f32[64]{0:T(128)S(1)} %fusion.22), channel_id=1, source_target_pairs={{1,0},{2,1},{3,2},{4,3},{5,4},{6,5},{7,6},{8,7},{9,8},{10,9},{11,1... | collective-permute-start | bytes 776 | tf_op jit(solution)/shard_map/ppermute | solution.py:21
  316.4 9.7 %collective-permute-start.2 = (f32[64]{0:T(128)S(1)}, f32[64]{0:T(128)S(1)}, u32[]{:S(2)}, u32[]{:S(2)}) collective-permute-start(f32[64]{0:T(128)S(1)} %fusion.22), channel_id=1, source_target_pairs={{0,1},{1,2},{2,3},{3,4},{4,5},{5,6},{6,7},{7,8},{8,9},{9,10},{10,1... | collective-permute-start | bytes 776 | tf_op jit(solution)/shard_map/ppermute | solution.py:19
  364.7 3.2 collective-permute-start.4
  404.4 6.7 %collective-permute-start.5 = (f32[64]{0:T(128)S(1)}, f32[64]{0:T(128)S(1)}, u32[]{:S(2)}, u32[]{:S(2)}) collective-permute-start(f32[64]{0:T(128)S(1)} %fusion.20), channel_id=1, source_target_pairs={{32,0},{48,16},{64,32},{80,48},{96,64},{112,80},{128,96},{144,112}... | collective-permute-start | bytes 776 | tf_op jit(solution)/shard_map/ppermute | solution.py:31
  472.6 5.0 %copy-start.2 = (f32[1024,1024]{1,0:T(8,128)S(1)}, f32[1024,1024]{1,0:T(8,128)}, u32[]{:S(2)}) copy-start(f32[1024,1024]{1,0:T(8,128)} %all-gather.12.cloned.1.call-done) | copy-start | bytes 12582916
  (1 other events, 0.7 us)
Sparse Core Ops, SparseCore 0:
  11.0 70.2 all-gather.17
  87.0 66.6 all-gather.11
  157.2 66.6 all-gather.7
  226.8 66.6 all-gather.13
  296.9 66.9 all-gather.9
  366.7 66.9 all-gather.15
where the time goes:
time: 492 us
  waiting for transfers between devices  265 us (54%)
  blocking collectives  111 us (23%)
  matrix products  62.9 us (13%)
  between operations  24.7 us (5%)
  starting transfers between devices  18.8 us (4%)
  local copies, waits for them, and re-layouts  6.74 us (1%)
    unnamed x3, blocking collectives  111 us
    all_gather x1, waiting for transfers between devices, body(): lax.all_gather(precision[0], 'row', axis=0, tiled=True)  62.7 us
    all_gather x1, waiting for transfers between devices, body(): lax.all_gather(gain_rows, 'row', axis=0, tiled=True)  59.8 us
    all_gather x2, waiting for transfers between devices, body(): lax.all_gather(piece_gain, 'row', axis=0, tiled=True)  57.4 us
    all_gather x2, waiting for transfers between devices, body(): lax.all_gather(piece_spread, 'row', axis=0, tiled=True)  52.6 us
    dot_general x11, matrix products, product(): jnp.dot(left, right, precision=HIGHEST, preferred_element_type=jnp.float32)  45.4 us
    ppermute x6, waiting for transfers between devices, shifted(): return lax.ppermute(block, axis, route)  31.6 us
    dot_general x3, matrix products, against(): lax.dot_general(left, right, (((1,), (1,)), ((), ())), precision=HIGHEST,...  17.6 us
  transfers between devices with their start and end apart: 14, of which 10 were waited for; matrix products, arithmetic and copies ran while one was open for 11% of the time, Pallas kernels for 0%

commit v1 on v0

--- a/solution.py
+++ b/solution.py
@@ -6,6 +6,13 @@
 NBAND = 5
 REACH = 64
 HIGHEST = lax.Precision.HIGHEST
+
+
+def exchange_gather(x, mesh_axis, dim):
+    size = lax.axis_size(mesh_axis)
+    blocks = jnp.stack([x for _ in range(size)])
+    blocks = lax.all_to_all(blocks, mesh_axis, split_axis=0, concat_axis=0)
+    return jnp.concatenate(blocks, axis=dim)
 
 
 def padded_2(cells, sides, width):
@@ -75,7 +82,7 @@
             rimmed, start_at, local_rows, 0
         )
     gain_full, forward_full = (
-        lax.all_gather(gain_rows, "row", axis=0, tiled=True),
+        exchange_gather(gain_rows, "row", 0),
         lax.all_gather(forward, "row", axis=0, tiled=True),
     )
     spread_now = spread_rows - against(crossed, gain_full)

time: 492 us -> 457 us (0.929)
  waiting for transfers between devices: 265 us -> 168 us
  blocking collectives: 111 us -> 171 us
    all_to_all x0 -> x1, blocking collectives: none -> 60 us  [exchange_gather(): blocks = lax.all_to_all(blocks, mesh_axis, split_axis=0, concat_axis=0)]
    all_gather x1 -> x0, waiting for transfers between devices: 59.8 us -> none  [body(): lax.all_gather(gain_rows, 'row', axis=0, tiled=True)]
    all_gather x2, waiting for transfers between devices: 57.4 us -> 20.2 us  [body(): lax.all_gather(piece_gain, 'row', axis=0, tiled=True)]
  transfers between devices with their start and end apart: 14 -> 13, of which waited for: 10 -> 9; matrix products, arithmetic and copies ran while one was open for 11% -> 11% of each run, Pallas kernels for 0% -> 0%
where the time goes in v1:
time: 457 us; the launch traced here: 456 us
  blocking collectives  171 us (37%)
  waiting for transfers between devices  168 us (37%)
  matrix products  60.1 us (13%)
  between operations  24.4 us (5%)
  starting transfers between devices  20.7 us (5%)
  local copies, waits for them, and re-layouts  9.21 us (2%)
    unnamed x3, blocking collectives  111 us
    all_gather x1, waiting for transfers between devices, body(): lax.all_gather(precision[0], 'row', axis=0, tiled=True)  62.7 us
    all_to_all x1, blocking collectives, exchange_gather(): blocks = lax.all_to_all(blocks, mesh_axis, split_axis=0, concat_axis=0)  60 us
    all_gather x2, waiting for transfers between devices, body(): lax.all_gather(piece_spread, 'row', axis=0, tiled=True)  53.3 us
    dot_general x11, matrix products, product(): jnp.dot(left, right, precision=HIGHEST, preferred_element_type=jnp.float32)  44.7 us
    ppermute x6, waiting for transfers between devices, shifted(): return lax.ppermute(block, axis, route)  31.2 us
    all_gather x2, waiting for transfers between devices, body(): lax.all_gather(piece_gain, 'row', axis=0, tiled=True)  20.2 us
    dot_general x3, matrix products, against(): lax.dot_general(left, right, (((1,), (1,)), ((), ())), precision=HIGHEST,...  15.4 us
  transfers between devices with their start and end apart: 13, of which 9 were waited for; matrix products, arithmetic and copies ran while one was open for 11% of the time, Pallas kernels for 0%

profile of v1, /device:TPU:96, one launch (start us, length us, event | category | flops | bytes accessed | tf_op | source)
XLA Modules:
  0.0 456.1 jit_solution(7597621127712083354)
XLA Ops:
  18.6 62.7 %all-gather.15.cloned.1.call-done = f32[1,1024,1024]{2,1,0:T(8,128)} async-done(((f32[1,64,1024]{2,1,0:T(8,128)}), f32[1,1024,1024]{2,1,0:T(8,128)}) %all-gather.15.cloned.1.call-update) | async-done | bytes 4194320 | tf_op jit(solution)/shard_map/all_gather | solution.py:70
  81.3 4.8 %fusion = f32[64,1024]{1,0:T(8,128)S(1)} fusion(f32[64,1024]{1,0:T(8,128)S(1)} %fusion.27, f32[1,1024,1024]{2,1,0:T(8,128)} %all-gather.15.cloned.1.call-done), kind=kOutput, calls=%fused_computation | convolution fusion | flops 805306368 | bytes 4718592 | tf_op jit(solution)/shard_map/dot_general | solution.py:42
  88.1 3.9 collective-permute-done
  93.2 60.0 %all_to_all.5 = f32[16,64,1024]{2,1,0:T(8,128)S(1)} all-to-all(f32[16,64,1024]{2,1,0:T(8,128)S(1)} %stack.2), channel_id=1, replica_groups=mesh['tm'=32,'row'=16] {'row'}, dimensions={0} | all-to-all | bytes 8388608 | tf_op jit(solution)/shard_map/all_to_all | solution.py:14
  155.2 4.1 convolution_subtract_fusion
  159.3 3.8 collective-permute-start.6
  163.1 3.9 collective-permute-done.6
  167.7 20.2 %all-gather.7.cloned.1.call-done = f32[1024,1024]{1,0:T(8,128)} async-done(((f32[64,1024]{1,0:T(8,128)}), f32[1024,1024]{1,0:T(8,128)}) %all-gather.7.cloned.1.call-update) | async-done | bytes 4194320 | tf_op jit(solution)/shard_map/all_gather | solution.py:97
  188.0 4.8 %convolution_select_fusion.1 = f32[64,1024]{1,0:T(8,128)S(1)} fusion(f32[64,1024]{1,0:T(8,128)S(1)} %fusion, f32[1024,1024]{1,0:T(8,128)} %all-gather.7.cloned.1.call-done, pred[]{:T(512)S(6)} %lt.30), kind=kOutput, calls=%fused_computation.6 | convolution fusion | flops 805371904 | bytes 4718593 | tf_op jit(solution)/shard_map/dot_general | solution.py:42
  192.8 2.4 collective-permute-start.1
  195.2 8.8 %collective-permute-done.1 = f32[64,1024]{1,0:T(8,128)S(1)} collective-permute-done((f32[64,1024]{1,0:T(8,128)S(1)}, f32[64,1024]{1,0:T(8,128)S(1)}, u32[]{:S(2)}, u32[]{:S(2)}) %collective-permute-start.1) | collective-permute-done | bytes 262176 | tf_op jit(solution)/shard_map/ppermute | solution.py:38
  205.0 53.3 %all-gather.11.cloned.1.call-done = f32[1024,1024]{1,0:T(8,128)} async-done(((f32[64,1024]{1,0:T(8,128)}), f32[1024,1024]{1,0:T(8,128)}) %all-gather.11.cloned.1.call-update) | async-done | bytes 4194320 | tf_op jit(solution)/shard_map/all_gather | solution.py:99
  258.2 5.0 %fusion.52 = f32[64,1024]{1,0:T(8,128)S(1)} fusion(f32[64,1024]{1,0:T(8,128)S(1)} %fusion, f32[1024,1024]{1,0:T(8,128)} %all-gather.11.cloned.1.call-done), kind=kOutput, calls=%fused_computation.67 | convolution fusion | flops 805306368 | bytes 4718592 | tf_op jit(solution)/shard_map/dot_general | solution.py:42
  263.2 4.1 fusion.6
  269.7 8.8 %collective-permute-done.7 = f32[64,1024]{1,0:T(8,128)S(1)} collective-permute-done((f32[64,1024]{1,0:T(8,128)S(1)}, f32[64,1024]{1,0:T(8,128)S(1)}, u32[]{:S(2)}, u32[]{:S(2)}) %collective-permute-start.7) | collective-permute-done | bytes 262176 | tf_op jit(solution)/shard_map/ppermute | solution.py:38
  281.2 4.5 collective-permute-start.2
  291.9 37.3 %all-reduce.1 = f32[1024]{0:T(1024)S(1)} all-reduce(f32[1024]{0:T(1024)S(1)} %fusion.37), channel_id=1, replica_groups=mesh['tm'=32,'row'=16] {'row'}, use_global_device_ids=true, to_apply=%add.1 | all-reduce | flops 1024 | bytes 8192
  332.9 36.0 %all-reduce.2 = f32[1024]{0:T(1024)S(1)} all-reduce(f32[1024]{0:T(1024)S(1)} %dynamic-update-slice.1), channel_id=1, replica_groups=mesh['tm'=32,'row'=16] {'row'}, use_global_device_ids=true, to_apply=%add.2 | all-reduce | flops 1024 | bytes 8192
  371.2 4.7 %collective-permute-done.5 = f32[64]{0:T(128)S(1)} collective-permute-done((f32[64]{0:T(128)S(1)}, f32[64]{0:T(128)S(1)}, u32[]{:S(2)}, u32[]{:S(2)}) %collective-permute-start.5) | collective-permute-done | bytes 288 | tf_op jit(solution)/shard_map/ppermute | solution.py:38
  376.1 37.4 %all-reduce.3 = f32[1024]{0:T(1024)S(1)} all-reduce(f32[1024]{0:T(1024)S(1)} %dynamic-update-slice.2), channel_id=1, replica_groups=mesh['tm'=32,'row'=16] {'row'}, use_global_device_ids=true, to_apply=%add.3 | all-reduce | flops 1024 | bytes 8192
  414.3 17.6 %fusion.54 = f32[1024,1024]{1,0:T(8,128)} fusion(f32[1024,1024]{1,0:T(8,128)} %bitcast.132, f32[1024,1024]{1,0:T(8,128)} %all-gather.7.cloned.1.call-done), kind=kOutput, calls=%fused_computation.69 | convolution fusion | flops 12884901888 | bytes 12582912 | tf_op jit(solution)/shard_map/dot_general | solution.py:42
  431.9 5.5 %fusion.5 = f32[1,64,1024]{2,1,0:T(8,128)} fusion(f32[64,1024]{1,0:T(8,128)S(1)} %convolution_select_fusion.1, f32[1024,1024]{1,0:T(8,128)} %all-gather.9.cloned.1.call-done, pred[]{:T(512)S(6)} %lt.29), kind=kOutput, calls=%fused_computation.7 | convolution fusion | flops 805371904 | bytes 4718593 | tf_op jit(solution)/shard_map/dot_general | solution.py:42
  437.4 5.0 %fusion.53 = f32[64,1024]{1,0:T(8,128)S(1)} fusion(f32[64,1024]{1,0:T(8,128)S(1)} %convolution_select_fusion.1, f32[1024,1024]{1,0:T(8,128)} %all-gather.13.cloned.1.call-done), kind=kOutput, calls=%fused_computation.68 | convolution fusion | flops 805306368 | bytes 4718592 | tf_op jit(solution)/shard_map/dot_general | solution.py:42
  442.4 7.2 %fusion.13 = f32[1,64,1024]{2,1,0:T(8,128)} fusion(f32[64,1024]{1,0:T(8,128)S(1)} %fusion.6, f32[64,1024]{1,0:T(8,128)S(1)} %fusion.53, f32[1024,1024]{1,0:T(8,128)} %fusion.54, f32[1024,1024]{1,0:T(8,128)S(1)} %bitcast.134, pred[]{:T(512)S(6)} %lt.30, pred[]{:T(512)S(6)} %lt.29), kind=kOutput, calls=%fused_computation.13 | convolution fusion | flops 806486016 | bytes 9175042 | tf_op jit(solution)/shard_map/dot_general | solution.py:46
  (59 shorter events, 26.0 us)
Async XLA Ops:
  7.2 272.1 %copy-start = (f32[1,128]{1,0:T(1,128)S(1)}, f32[1,128]{1,0:T(1,128)}, u32[]{:S(2)}) copy-start(f32[1,128]{1,0:T(1,128)} %param.12) | copy-start | bytes 1540
  7.2 74.1 %all-gather.15.cloned.1.call-start = ((), (), s32[]{:S(2)}) async-start(), calls=%async_computation.5 | async-start | bytes 4456448 | tf_op jit(solution)/shard_map/all_gather | solution.py:70
  7.9 180.1 %all-gather.7.cloned.1.call-start = ((), (), s32[]{:S(2)}) async-start(), calls=%async_computation.1 | async-start | bytes 4456448 | tf_op jit(solution)/shard_map/all_gather | solution.py:97
  86.1 5.8 %collective-permute-start = (f32[64,1024]{1,0:T(8,128)S(1)}, f32[64,1024]{1,0:T(8,128)S(1)}, u32[]{:S(2)}, u32[]{:S(2)}) collective-permute-start(f32[64,1024]{1,0:T(8,128)S(1)} %fusion), channel_id=1, source_target_pairs={{16,0},{32,16},{48,32},{64,48},{80,64},{96,80},{112,96},{128,112},... | collective-permute-start | bytes 786440 | tf_op jit(solution)/shard_map/ppermute | solution.py:38
  91.9 0.7 copy-start.7
  92.6 165.6 %all-gather.11.cloned.1.call-start = ((), (), s32[]{:S(2)}) async-start(), calls=%async_computation.3 | async-start | bytes 4456448 | tf_op jit(solution)/shard_map/all_gather | solution.py:99
  93.2 62.0 %copy-start.4 = (f32[1,64,1024]{2,1,0:T(8,128)S(1)}, f32[1,64,1024]{2,1,0:T(8,128)}, u32[]{:S(2)}) copy-start(f32[1,64,1024]{2,1,0:T(8,128)} %param.7) | copy-start | bytes 786436
  153.2 2.0 copy-start.1
  159.3 7.7 %collective-permute-start.6 = (f32[64,1024]{1,0:T(8,128)S(1)}, f32[64,1024]{1,0:T(8,128)S(1)}, u32[]{:S(2)}, u32[]{:S(2)}) collective-permute-start(f32[64,1024]{1,0:T(8,128)S(1)} %convolution_subtract_fusion), channel_id=1, source_target_pairs={{16,0},{32,16},{48,32},{64,48},{80,64},{96,80},{112,96},{128,112},... | collective-permute-start | bytes 786440 | tf_op jit(solution)/shard_map/ppermute | solution.py:38
  167.0 0.7 copy-start.8
  167.7 264.2 %all-gather.9.cloned.1.call-start = ((), (), s32[]{:S(2)}) async-start(), calls=%async_computation.2 | async-start | bytes 4456448 | tf_op jit(solution)/shard_map/all_gather | solution.py:97
  192.8 11.2 %collective-permute-start.1 = (f32[64,1024]{1,0:T(8,128)S(1)}, f32[64,1024]{1,0:T(8,128)S(1)}, u32[]{:S(2)}, u32[]{:S(2)}) collective-permute-start(f32[64,1024]{1,0:T(8,128)S(1)} %convolution_select_fusion.1), channel_id=1, source_target_pairs={{32,0},{48,16},{64,32},{80,48},{96,64},{112,80},{128,96},{144,112}... | collective-permute-start | bytes 786440 | tf_op jit(solution)/shard_map/ppermute | solution.py:38
  204.0 0.7 copy-start.5
  204.7 74.5 %copy-start.10 = (s32[1,128]{1,0:T(1,128)S(1)}, s32[1,128]{1,0:T(1,128)}, u32[]{:S(2)}) copy-start(s32[1,128]{1,0:T(1,128)} %param.13) | copy-start | bytes 1540
  204.7 74.9 %copy-start.9 = (f32[1,64]{1,0:T(1,128)S(1)}, f32[1,64]{1,0:T(1,128)}, u32[]{:S(2)}) copy-start(f32[1,64]{1,0:T(1,128)} %param.11) | copy-start | bytes 772
  204.7 232.7 %all-gather.13.cloned.1.call-start = ((), (), s32[]{:S(2)}) async-start(), calls=%async_computation.4 | async-start | bytes 4456448 | tf_op jit(solution)/shard_map/all_gather | solution.py:99
  258.2 5.0 %copy-start.2 = (f32[16,64,1024]{2,1,0:T(8,128)S(1)}, f32[16,64,1024]{2,1,0:T(8,128)}, u32[]{:S(2)}) copy-start(f32[16,64,1024]{2,1,0:T(8,128)} %copy-done.1) | copy-start | bytes 12582916
  267.4 11.1 %collective-permute-start.7 = (f32[64,1024]{1,0:T(8,128)S(1)}, f32[64,1024]{1,0:T(8,128)S(1)}, u32[]{:S(2)}, u32[]{:S(2)}) collective-permute-start(f32[64,1024]{1,0:T(8,128)S(1)} %fusion.6), channel_id=1, source_target_pairs={{32,0},{48,16},{64,32},{80,48},{96,64},{112,80},{128,96},{144,112}... | collective-permute-start | bytes 786440 | tf_op jit(solution)/shard_map/ppermute | solution.py:38
  278.5 0.7 copy-start.6
  279.9 11.1 %collective-permute-start.3 = (f32[64]{0:T(128)S(1)}, f32[64]{0:T(128)S(1)}, u32[]{:S(2)}, u32[]{:S(2)}) collective-permute-start(f32[64]{0:T(128)S(1)} %fusion.22), channel_id=1, source_target_pairs={{1,0},{2,1},{3,2},{4,3},{5,4},{6,5},{7,6},{8,7},{9,8},{10,9},{11,1... | collective-permute-start | bytes 776 | tf_op jit(solution)/shard_map/ppermute | solution.py:28
  281.2 9.7 %collective-permute-start.2 = (f32[64]{0:T(128)S(1)}, f32[64]{0:T(128)S(1)}, u32[]{:S(2)}, u32[]{:S(2)}) collective-permute-start(f32[64]{0:T(128)S(1)} %fusion.22), channel_id=1, source_target_pairs={{0,1},{1,2},{2,3},{3,4},{4,5},{5,6},{6,7},{7,8},{8,9},{9,10},{10,1... | collective-permute-start | bytes 776 | tf_op jit(solution)/shard_map/ppermute | solution.py:26
  329.5 3.2 collective-permute-start.4
  369.2 6.7 %collective-permute-start.5 = (f32[64]{0:T(128)S(1)}, f32[64]{0:T(128)S(1)}, u32[]{:S(2)}, u32[]{:S(2)}) collective-permute-start(f32[64]{0:T(128)S(1)} %fusion.20), channel_id=1, source_target_pairs={{32,0},{48,16},{64,32},{80,48},{96,64},{112,80},{128,96},{144,112}... | collective-permute-start | bytes 776 | tf_op jit(solution)/shard_map/ppermute | solution.py:38
  437.4 5.0 %copy-start.3 = (f32[16,64,1024]{2,1,0:T(8,128)S(1)}, f32[16,64,1024]{2,1,0:T(8,128)}, u32[]{:S(2)}) copy-start(f32[16,64,1024]{2,1,0:T(8,128)} %copy-done.1) | copy-start | bytes 12582916
Sparse Core Ops, SparseCore 0:
  11.0 70.2 all-gather.14
  92.8 95.1 all-gather.6
  191.6 66.6 all-gather.10
  261.7 66.9 all-gather.8
  331.6 66.9 all-gather.12
